TPU v7x, 32 devices: a whole 2x2x4 slice. The times are simulated.
32 devices in a mesh: grp: 4 (over z), dev: 8 (over y, x, core).
Axes of the slice: x: 2, y: 2, z: 4, core: 2. Of those that a mesh axis runs over, the one named last changes fastest.
Arguments:
- adjoint_load: float32 [1024, 64, 128], P(('grp', 'dev')), as said below
- local_ops: float32 [4, 2016, 64, 64], P(None, ('grp', 'dev')), as said below
- coarse_ops: float32 [4, 4, 7, 64, 64], P(None, 'grp'), as said below
- slab_order: int32 [32, 32], P(('grp', 'dev')), may hold values from 0 to 31, each once within a row
Outputs:
- slab_adjoint: float32 [1024, 64, 128], P(('grp', 'dev'))
Inputs may be any that keep to these rules, and one draw needn't show every extreme that they name: `local_ops`: blocks of kind 3 approximate the inverses of the diagonal blocks. `coarse_ops`: same four kinds of blocks as local_ops. `adjoint_load`: real-valued right-hand sides. `slab_order`: each row lists every one of the 32 rows of one device once.
All inputs are finite; a program needn't handle non-finite values.
Results may differ from a plain program's by a relative error of at most 0.0001.
Values sent between devices are 32-bit elements; how exact they have to be, the bound alone decides.
A program may use at most 64 MiB of HBM per device.

v0:
```python
import functools
import jax
import jax.numpy as jnp
from jax import lax
from jax.experimental import pallas as pl
from jax.experimental.pallas import tpu as pltpu
from jax.sharding import PartitionSpec as P

damping = 0.8
GROUP = 4
CHUNKS = 4
f32 = jnp.float32
bf16 = jnp.bfloat16


def split(value):
    high = value.astype(bf16)
    return high, (value - high.astype(f32)).astype(bf16)


def over_rows(low, high, body, group=GROUP):
    full = (high - low) // group
    if full > 1:
        def step(index, carry):
            body([low + index * group + t for t in range(group)])
            return carry
        lax.fori_loop(0, full, step, 0)
        low += full * group
    while low < high:
        body(list(range(low, min(low + group, high))))
        low += group


def kernel(
    plan,
    load, ops, coarse, order,
    out,
    raw, raw_s, raw_a, raw_g, raw_c,
    a_hi, a_lo, s3, b, x, e, x_hi, x_lo, f_hi, f_lo, staged,
    local_sem, b_send, b_recv, o_send, o_recv, go_send, go_recv, g_send, g_recv, t_send, t_recv,
):
    devices, groups, heights, bases, wide, wide_bases = plan
    levels = len(heights)
    rows = heights[0]
    per_slab = rows // groups
    dev = lax.axis_index("dev")
    grp = lax.axis_index("grp")
    has = (dev > 0, dev < devices - 1)
    offsets = [2 * rows - 2 * rows // 2**l for l in range(levels + 1)]
    gather_base = wide_bases[0]

    local = []

    def fetch(src, dst):
        copy = pltpu.make_async_copy(src, dst, local_sem.at[len(local)])
        copy.start()
        local.append(copy)
        return copy

    load_copy = fetch(load, b.at[0, pl.ds(bases[0] + 2, rows)])
    piece = rows // CHUNKS
    fine_copies = [
        fetch(ops.at[:, pl.ds(c * piece, piece)], raw.at[:, pl.ds(c * piece, piece)])
        for c in range(CHUNKS)
    ]
    rest = ops.shape[1] - rows
    rest_copy = fetch(ops.at[:, pl.ds(rows, rest)], raw.at[:, pl.ds(rows, rest)])
    coarse_copy = fetch(coarse, raw_c)

    barrier = pltpu.get_barrier_semaphore()
    for k in range(1, devices):
        pl.semaphore_signal(barrier, inc=1, device_id={"dev": lax.rem(dev + k, devices)},
                            device_id_type=pl.DeviceIdType.MESH)
    for k in range(1, groups):
        pl.semaphore_signal(barrier, inc=1, device_id={"grp": lax.rem(grp + k, groups)},
                            device_id_type=pl.DeviceIdType.MESH)
    pl.semaphore_wait(barrier, devices - 1 + groups - 1)

    def remote(src, dst, send, recv, axis, target):
        return pltpu.make_async_remote_copy(
            src_ref=src, dst_ref=dst, send_sem=send, recv_sem=recv,
            device_id={axis: target}, device_id_type=pl.DeviceIdType.MESH)

    def b_halo(cycle, l, side):
        n, base = heights[l], bases[l]
        start = n - 2 if side == 0 else 0
        if cycle == 0 and l == 0:
            src = load.at[pl.ds(start, 2)]
        else:
            src = b.at[cycle, pl.ds(base + 2 + start, 2)]
        dst = b.at[cycle, pl.ds(base + (0 if side == 0 else n + 2), 2)]
        target = dev + 1 if side == 0 else dev - 1
        return remote(src, dst, b_send.at[cycle, l, side], b_recv.at[cycle, l, side], "dev", target)

    def o_halo(l, side, part):
        n = heights[l]
        if part == 0:
            start = n - 2 if side == 0 else 0
            src, dst = ops.at[pl.ds(3, 1), pl.ds(offsets[l] + start, 2)], raw_s.at[l, side]
        else:
            start = n - 1 if side == 0 else 0
            src, dst = ops.at[pl.ds(0, 3), pl.ds(offsets[l] + start, 1)], raw_a.at[l, side]
        target = dev + 1 if side == 0 else dev - 1
        return remote(src, dst, o_send.at[l, side, part], o_recv.at[l, side, part], "dev", target)

    def on_send(side, act):
        pl.when(has[1 - side])(act)

    def send_b(cycle, l):
        for side in range(2):
            on_send(side, lambda side=side: b_halo(cycle, l, side).start())

    def go_copy(k, sender, target):
        return remote(ops.at[:, pl.ds(offsets[levels], 1)], raw_g.at[sender],
                      go_send.at[k], go_recv.at[sender], "dev", target)

    def g_copy(cycle, k, sender, target):
        row = b.at[cycle, pl.ds(gather_base + 2 + sender, 1)]
        return remote(row, row, g_send.at[cycle, k], g_recv.at[cycle, sender], "dev", target)

    send_b(0, 0)
    for l in range(levels):
        for side in range(2):
            def begin(side=side, l=l):
                o_halo(l, side, 0).start()
                o_halo(l, side, 1).start()
            on_send(side, begin)
    for k in range(1, devices):
        go_copy(k, dev, lax.rem(dev + k, devices)).start()

    def pack_s(row, block):
        hi, lo = split(damping * block)
        hi, lo = hi.astype(f32), lo.astype(f32)
        s3[row] = jnp.concatenate([hi, hi, lo], axis=1).astype(bf16)

    def pack_a(row, lower, middle, upper):
        hi, lo = split(jnp.concatenate([lower, middle, upper], axis=1))
        a_hi[row] = hi
        a_lo[row] = lo

    def pack_own(l, low, high):
        def body(js):
            for j in js:
                source = offsets[l] + j
                row = bases[l] + 2 + j
                pack_a(row, raw[0, source], raw[1, source], raw[2, source])
                pack_s(row, raw[3, source])
        over_rows(low, high, body, 2)

    def s_mul(row, value):
        hi, lo = split(value)
        return jnp.dot(s3[row], jnp.concatenate([hi, lo, hi], axis=0), preferred_element_type=f32)

    def a_mul(row, j, hi_ref, lo_ref):
        hi = hi_ref[pl.ds(j - 1, 3)].reshape(-1, hi_ref.shape[-1])
        lo = lo_ref[pl.ds(j - 1, 3)].reshape(-1, lo_ref.shape[-1])
        high = a_hi[row]
        return (jnp.dot(high, lo, preferred_element_type=f32)
                + jnp.dot(a_lo[row], hi, preferred_element_type=f32)
                + jnp.dot(high, hi, preferred_element_type=f32))

    def presmooth(cycle, base, low, high):
        def body(js):
            values = [s_mul(base + j, b[cycle, base + j]) for j in js]
            halves = [split(v) for v in values]
            for j, v, (hi, lo) in zip(js, values, halves):
                x[base + j] = v
                x_hi[j] = hi
                x_lo[j] = lo
        over_rows(low, high, body)

    def restrict(cycle, base, pairs, store):
        def body(ps):
            js = [j for p in ps for j in (2 + 2 * p, 3 + 2 * p)]
            r = [b[cycle, base + j] - a_mul(base + j, j, x_hi, x_lo) for j in js]
            for t, p in enumerate(ps):
                store(p, 0.5 * (r[2 * t] + r[2 * t + 1]))
        for low, high in pairs:
            over_rows(low, high, body, 2)

    def correct(base, low, high, e_row):
        def body(ps):
            vs = []
            for p in ps:
                add = e[e_row(p + 1)]
                vs += [x[base + 2 * p] + add, x[base + 2 * p + 1] + add]
            halves = [split(v) for v in vs]
            js = [j for p in ps for j in (2 * p, 2 * p + 1)]
            for j, v, (hi, lo) in zip(js, vs, halves):
                x[base + j] = v
                x_hi[j] = hi
                x_lo[j] = lo
        over_rows(low // 2, high // 2, body, 2)

    def smoothed(cycle, base, js):
        r = [b[cycle, base + j] - a_mul(base + j, j, x_hi, x_lo) for j in js]
        return [x[base + j] + s_mul(base + j, v) for j, v in zip(js, r)]

    def postsmooth(cycle, base, low, high, keep=False):
        def body(js):
            values = smoothed(cycle, base, js)
            for j, v in zip(js, values):
                e[base + j] = v
            if keep:
                for j, v in zip(js, values):
                    f_hi[j], f_lo[j] = split(v)
        over_rows(low, high, body)

    def zero_rows(ref, indices):
        for i in indices:
            ref[i] = jnp.zeros(ref.shape[1:], ref.dtype)

    def down_local(cycle, l):
        n, base = heights[l], bases[l]
        if cycle == 0:
            if l == 0:
                load_copy.wait()
                for c in range(CHUNKS):
                    fine_copies[c].wait()
                    pack_own(0, c * piece, (c + 1) * piece)
            else:
                if l == 1:
                    rest_copy.wait()
                pack_own(l, 0, n)
        presmooth(cycle, base, 2, n + 2)
        for side in range(2):
            outer = (0, 1) if side == 0 else (n + 2, n + 3)
            inner = 1 if side == 0 else n + 2

            def arrive(side=side, outer=outer, inner=inner):
                b_halo(cycle, l, side).wait_recv()
                if cycle == 0:
                    o_halo(l, side, 0).wait_recv()
                    o_halo(l, side, 1).wait_recv()
                    for t, j in enumerate(outer):
                        pack_s(base + j, raw_s[l, side, 0, t])
                    pack_a(base + inner, raw_a[l, side, 0, 0], raw_a[l, side, 1, 0], raw_a[l, side, 2, 0])

            pl.when(has[side])(arrive)
            if cycle == 0:
                def blank(outer=outer, inner=inner):
                    for j in outer:
                        s3[base + j] = jnp.zeros(s3.shape[1:], bf16)
                        b[0, base + j] = jnp.zeros(b.shape[2:], f32)
                        b[1, base + j] = jnp.zeros(b.shape[2:], f32)
                    a_hi[base + inner] = jnp.zeros(a_hi.shape[1:], bf16)
                    a_lo[base + inner] = jnp.zeros(a_lo.shape[1:], bf16)
                pl.when(jnp.logical_not(has[side]))(blank)
        js = [0, 1, n + 2, n + 3]
        values = [s_mul(base + j, b[cycle, base + j]) for j in js]
        for j, v in zip(js, values):
            x[base + j] = v
            x_hi[j], x_lo[j] = split(v)
        half = n // 2
        if l + 1 < levels:
            def store(p, c):
                b[cycle, bases[l + 1] + 2 + p] = c
            if half > 4:
                restrict(cycle, base, [(0, 2), (half - 2, half)], store)
                send_b(cycle, l + 1)
                restrict(cycle, base, [(2, half - 2)], store)
            else:
                restrict(cycle, base, [(0, half)], store)
                send_b(cycle, l + 1)
        else:
            def store(p, c):
                b[cycle, gather_base + 2 + dev] = c
            restrict(cycle, base, [(0, half)], store)
            for k in range(1, devices):
                g_copy(cycle, k, dev, lax.rem(dev + k, devices)).start()

    def solve_wide(cycle):
        if cycle == 0:
            own = offsets[levels]
            pack_a(gather_base + 2 + dev, raw[0, own], raw[1, own], raw[2, own])
            pack_s(gather_base + 2 + dev, raw[3, own])
            coarse_copy.wait()
            first = 0
            for m in range(1, len(wide)):
                def body(js, first=first, m=m):
                    for j in js:
                        row = wide_bases[m] + 2 + j
                        pack_a(row, raw_c[0, 0, first + j], raw_c[1, 0, first + j], raw_c[2, 0, first + j])
                        pack_s(row, raw_c[3, 0, first + j])
                over_rows(0, wide[m], body, 2)
                first += wide[m]

            def take(k, carry):
                sender = lax.rem(dev + k, devices)
                go_copy(0, sender, sender).wait_recv()
                row = gather_base + 2 + sender
                pack_a(row, raw_g[sender, 0, 0], raw_g[sender, 1, 0], raw_g[sender, 2, 0])
                pack_s(row, raw_g[sender, 3, 0])
                return carry
            lax.fori_loop(1, devices, take, 0)
            zero_rows(e, [gather_base + 1, gather_base + wide[0] + 2])
        for k in range(1, devices):
            sender = lax.rem(dev + k, devices)
            g_copy(cycle, 0, sender, sender).wait_recv()

        def visit(m):
            n, base = wide[m], wide_bases[m]
            pads = [1, n + 2]
            presmooth(cycle, base, 2, n + 2)
            if m + 1 < len(wide):
                zero_rows(x_hi, pads)
                zero_rows(x_lo, pads)

                def store(p, c):
                    b[cycle, wide_bases[m + 1] + 2 + p] = c
                restrict(cycle, base, [(0, n // 2)], store)
                visit(m + 1)
                correct(base, 2, n + 2, lambda i: wide_bases[m + 1] + i)
            zero_rows(x_hi, pads)
            zero_rows(x_lo, pads)
            postsmooth(cycle, base, 2, n + 2)
        visit(0)

    def up_to(cycle, l):
        if l == levels - 1:
            correct(bases[l], 0, heights[l] + 4, lambda i: gather_base + dev + i)
        else:
            correct(bases[l], 0, heights[l] + 4, lambda i: bases[l + 1] + i)

    for l in range(levels):
        down_local(0, l)
    solve_wide(0)
    for l in reversed(range(levels)):
        up_to(0, l)
        postsmooth(0, bases[l], 1, heights[l] + 3, keep=l == 0)

    base = bases[0]

    def again(js):
        values = [b[0, base + j] - a_mul(base + j, j, f_hi, f_lo) for j in js]
        for j, v in zip(js, values):
            b[1, base + j] = v
    again([2, 3, rows, rows + 1])
    send_b(1, 0)
    over_rows(4, rows, again)

    for l in range(levels):
        down_local(1, l)
    solve_wide(1)
    for l in reversed(range(1, levels)):
        up_to(1, l)
        postsmooth(1, bases[l], 1, heights[l] + 3)
    up_to(1, 0)

    def slab_copy(k, slab, sender):
        return remote(staged.at[pl.ds(slab * per_slab, per_slab)], out.at[pl.ds(sender * per_slab, per_slab)],
                      t_send.at[k], t_recv.at[sender], "grp", slab)

    steps = [(k + groups // 2) % groups for k in range(groups)]
    steps = [k for k in steps if k] + [0]
    for k in steps:
        slab = lax.rem(grp + k, groups)

        def body(us, slab=slab):
            ts = [slab * per_slab + u for u in us]
            js = [order[0, t] + 2 for t in ts]
            values = smoothed(1, base, js)
            values = [v + e[base + j] for v, j in zip(values, js)]
            for t, v in zip(ts, values):
                staged[t] = v
        over_rows(0, per_slab, body)
        if k:
            slab_copy(k, slab, grp).start()
        else:
            own = pltpu.make_async_copy(staged.at[pl.ds(slab * per_slab, per_slab)],
                                        out.at[pl.ds(grp * per_slab, per_slab)], local_sem.at[0])
            own.start()
            own.wait()

    for l in range(levels):
        for side in range(2):
            def left(l=l, side=side):
                b_halo(0, l, side).wait_send()
                b_halo(1, l, side).wait_send()
                o_halo(l, side, 0).wait_send()
                o_halo(l, side, 1).wait_send()
            on_send(side, left)
    for k in range(1, devices):
        target = lax.rem(dev + k, devices)
        go_copy(k, dev, target).wait_send()
        g_copy(0, k, dev, target).wait_send()
        g_copy(1, k, dev, target).wait_send()
    for k in range(1, groups):
        slab = lax.rem(grp + k, groups)
        slab_copy(k, slab, grp).wait_send()
        slab_copy(k, slab, slab).wait_recv()


def shards(adjoint_load, local_ops, coarse_ops, slab_order):
    rows, size, cases = adjoint_load.shape
    devices = lax.axis_size("dev")
    groups = lax.axis_size("grp")
    levels = rows.bit_length() - 1
    heights = [rows >> l for l in range(levels)]
    wide = [devices]
    while sum(wide[1:]) < coarse_ops.shape[2]:
        wide.append(wide[-1] // 2)
    bases, total = [], 0
    for n in heights + wide:
        bases.append(total)
        total += n + 4
    plan = (devices, groups, heights, bases[:levels], wide, bases[levels:])
    most = max(rows, devices) + 4
    kinds = local_ops.shape[0]
    dma = pltpu.SemaphoreType.DMA
    scratch = [
        pltpu.VMEM(local_ops.shape, f32),
        pltpu.VMEM((levels, 2, 1, 2, size, size), f32),
        pltpu.VMEM((levels, 2, 3, 1, size, size), f32),
        pltpu.VMEM((devices, kinds, 1, size, size), f32),
        pltpu.VMEM(coarse_ops.shape, f32),
        pltpu.VMEM((total, size, 3 * size), bf16),
        pltpu.VMEM((total, size, 3 * size), bf16),
        pltpu.VMEM((total, size, 3 * size), bf16),
        pltpu.VMEM((2, total, size, cases), f32),
        pltpu.VMEM((total, size, cases), f32),
        pltpu.VMEM((total, size, cases), f32),
        pltpu.VMEM((most, size, cases), bf16),
        pltpu.VMEM((most, size, cases), bf16),
        pltpu.VMEM((rows + 4, size, cases), bf16),
        pltpu.VMEM((rows + 4, size, cases), bf16),
        pltpu.VMEM((rows, size, cases), f32),
        dma((CHUNKS + 3,)),
        dma((2, levels, 2)), dma((2, levels, 2)),
        dma((levels, 2, 2)), dma((levels, 2, 2)),
        dma((devices,)), dma((devices,)),
        dma((2, devices)), dma((2, devices)),
        dma((groups,)), dma((groups,)),
    ]
    anywhere = pl.BlockSpec(memory_space=pl.ANY)
    return pl.pallas_call(
        functools.partial(kernel, plan),
        out_shape=jax.ShapeDtypeStruct(adjoint_load.shape, f32),
        in_specs=[anywhere, anywhere, anywhere, pl.BlockSpec(memory_space=pltpu.SMEM)],
        out_specs=anywhere,
        scratch_shapes=scratch,
        compiler_params=pltpu.CompilerParams(
            collective_id=0, has_side_effects=True, vmem_limit_bytes=62 * 2**20),
    )(adjoint_load, local_ops, coarse_ops, slab_order)


def solution(mesh):
    placed = (
        P(("grp", "dev"), None, None),
        P(None, ("grp", "dev"), None, None),
        P(None, "grp", None, None, None),
        P(("grp", "dev"), None),
    )
    return jax.shard_map(
        shards, mesh=mesh, in_specs=placed, out_specs=P(("grp", "dev"), None, None), check_vma=False
    )
```

profile of v0, /device:TPU:10, one launch (start us, length us, event | category | flops | bytes accessed | tf_op | source)
XLA Modules:
  0.0 131.5 jit_solution(10036233414139730432)
XLA Ops:
  0.0 129.2 %shard_map.46 = f32[32,64,128]{2,1,0:T(8,128)} custom-call(f32[32,64,128]{2,1,0:T(8,128)} %load.1, f32[4,63,64,64]{3,2,1,0:T(8,128)} %ops.1, f32[4,1,7,64,64]{4,3,2,1,0:T(8,128)} %coarse.1, s32[1,32]{1,0:T(1,128)} %order.1), custom_call_target="tpu_custom_call" | custom-call | tf_op jit(solution)/shard_map/pallas_call | solution.py:436
  129.2 2.3 %copy.6 = f32[32,64,128]{2,1,0:T(8,128)} copy(f32[32,64,128]{2,1,0:T(8,128)} %shard_map.46) | data formatting | bytes 2097152
where the time goes:
time: 132 us; the launch traced here: 131 us
  Pallas kernels  129 us (98%)
  local copies, waits for them, and re-layouts  2.31 us (2%)
    pallas_call x1, Pallas kernels, shards(): pl.pallas_call(functools.partial(kernel, plan), out_shape=jax.ShapeDtypeS...  129 us

commit v1 on v0

--- a/solution.py
+++ b/solution.py
@@ -36,7 +36,7 @@
     load, ops, coarse, order,
     out,
     raw, raw_s, raw_a, raw_g, raw_c,
-    a_hi, a_lo, s3, b, x, e, x_hi, x_lo, f_hi, f_lo, staged,
+    a_op, r_op, s4, b, x, first, x_two, f_two, staged,
     local_sem, b_send, b_recv, o_send, o_recv, go_send, go_recv, g_send, g_recv, t_send, t_recv,
 ):
     devices, groups, heights, bases, wide, wide_bases = plan
@@ -128,83 +128,124 @@
     for k in range(1, devices):
         go_copy(k, dev, lax.rem(dev + k, devices)).start()
 
+    size = x.shape[1]
+    cases = x.shape[2]
+
     def pack_s(row, block):
         hi, lo = split(damping * block)
         hi, lo = hi.astype(f32), lo.astype(f32)
-        s3[row] = jnp.concatenate([hi, hi, lo], axis=1).astype(bf16)
-
-    def pack_a(row, lower, middle, upper):
-        hi, lo = split(jnp.concatenate([lower, middle, upper], axis=1))
-        a_hi[row] = hi
-        a_lo[row] = lo
+        s4[row] = jnp.concatenate([hi, hi, lo, lo], axis=1).astype(bf16)
+
+    def placed_a(odd, lower, middle, upper):
+        none = jnp.zeros_like(middle)
+        blocks = [none, lower, middle, upper] if odd else [lower, middle, upper, none]
+        return jnp.concatenate(blocks, axis=1)
+
+    def put(ref, row, value):
+        hi, lo = split(value)
+        ref[row, pl.ds(0, size)] = hi
+        ref[row, pl.ds(size, size)] = lo
+
+    def pack_pair(base, p, blocks):
+        row = base + 2 + 2 * p
+        (l0, m0, u0, inv0), (l1, m1, u1, inv1) = blocks
+        even, odd = placed_a(False, l0, m0, u0), placed_a(True, l1, m1, u1)
+        put(a_op, row, even)
+        put(a_op, row + 1, odd)
+        put(r_op, base // 2 + 1 + p, 0.5 * (even + odd))
+        pack_s(row, inv0)
+        pack_s(row + 1, inv1)
 
     def pack_own(l, low, high):
-        def body(js):
-            for j in js:
-                source = offsets[l] + j
-                row = bases[l] + 2 + j
-                pack_a(row, raw[0, source], raw[1, source], raw[2, source])
-                pack_s(row, raw[3, source])
-        over_rows(low, high, body, 2)
+        def body(ps):
+            for p in ps:
+                source = offsets[l] + 2 * p
+                pack_pair(bases[l], p, [[raw[k, source + t] for k in range(4)] for t in range(2)])
+        over_rows(low // 2, high // 2, body, 2)
 
     def s_mul(row, value):
         hi, lo = split(value)
-        return jnp.dot(s3[row], jnp.concatenate([hi, lo, hi], axis=0), preferred_element_type=f32)
-
-    def a_mul(row, j, hi_ref, lo_ref):
-        hi = hi_ref[pl.ds(j - 1, 3)].reshape(-1, hi_ref.shape[-1])
-        lo = lo_ref[pl.ds(j - 1, 3)].reshape(-1, lo_ref.shape[-1])
-        high = a_hi[row]
-        return (jnp.dot(high, lo, preferred_element_type=f32)
-                + jnp.dot(a_lo[row], hi, preferred_element_type=f32)
-                + jnp.dot(high, hi, preferred_element_type=f32))
+        return jnp.dot(s4[row], jnp.concatenate([hi, lo, hi, lo], axis=0), preferred_element_type=f32)
+
+    def gathered(product):
+        upper, lower = product[:size], product[size:]
+        return (lower[:, cases:] + (upper[:, cases:] + lower[:, :cases])) + upper[:, :cases]
+
+    def window(ref, low):
+        return ref[pl.ds(low, 4)].reshape(4 * size, 2 * cases)
+
+    def a_pair(base, j, ref):
+        both = a_op[pl.ds(base + j, 2)].reshape(4 * size, 4 * size)
+        product = jnp.dot(both, window(ref, j - 1), preferred_element_type=f32)
+        return [gathered(product[: 2 * size]), gathered(product[2 * size :])]
+
+    def a_single(base, j, low, ref):
+        return gathered(jnp.dot(a_op[base + j], window(ref, low), preferred_element_type=f32))
+
+    def two(ref, j, value):
+        hi, lo = split(value)
+        ref[j, :, pl.ds(0, cases)] = hi
+        ref[j, :, pl.ds(cases, cases)] = lo
 
     def presmooth(cycle, base, low, high):
         def body(js):
             values = [s_mul(base + j, b[cycle, base + j]) for j in js]
-            halves = [split(v) for v in values]
-            for j, v, (hi, lo) in zip(js, values, halves):
+            for j, v in zip(js, values):
                 x[base + j] = v
-                x_hi[j] = hi
-                x_lo[j] = lo
-        over_rows(low, high, body)
+                two(x_two, j, v)
+        over_rows(low, high, body, 8)
 
     def restrict(cycle, base, pairs, store):
         def body(ps):
-            js = [j for p in ps for j in (2 + 2 * p, 3 + 2 * p)]
-            r = [b[cycle, base + j] - a_mul(base + j, j, x_hi, x_lo) for j in js]
-            for t, p in enumerate(ps):
-                store(p, 0.5 * (r[2 * t] + r[2 * t + 1]))
+            values = []
+            for p in ps:
+                j = 2 + 2 * p
+                product = jnp.dot(r_op[base // 2 + 1 + p], window(x_two, j - 1), preferred_element_type=f32)
+                values.append(0.5 * (b[cycle, base + j] + b[cycle, base + j + 1]) - gathered(product))
+            for p, v in zip(ps, values):
+                store(p, v)
         for low, high in pairs:
-            over_rows(low, high, body, 2)
+            over_rows(low, high, body, 4)
 
     def correct(base, low, high, e_row):
         def body(ps):
-            vs = []
+            js, vs = [], []
             for p in ps:
-                add = e[e_row(p + 1)]
+                add = x[e_row(p + 1)]
+                js += [2 * p, 2 * p + 1]
                 vs += [x[base + 2 * p] + add, x[base + 2 * p + 1] + add]
-            halves = [split(v) for v in vs]
-            js = [j for p in ps for j in (2 * p, 2 * p + 1)]
-            for j, v, (hi, lo) in zip(js, vs, halves):
+            for j, v in zip(js, vs):
                 x[base + j] = v
-                x_hi[j] = hi
-                x_lo[j] = lo
+                two(x_two, j, v)
         over_rows(low // 2, high // 2, body, 2)
 
-    def smoothed(cycle, base, js):
-        r = [b[cycle, base + j] - a_mul(base + j, j, x_hi, x_lo) for j in js]
+    def finish(cycle, base, js, products):
+        r = [b[cycle, base + j] - v for j, v in zip(js, products)]
         return [x[base + j] + s_mul(base + j, v) for j, v in zip(js, r)]
 
-    def postsmooth(cycle, base, low, high, keep=False):
-        def body(js):
-            values = smoothed(cycle, base, js)
-            for j, v in zip(js, values):
-                e[base + j] = v
+    def settle(base, js, values, keep):
+        for j, v in zip(js, values):
             if keep:
-                for j, v in zip(js, values):
-                    f_hi[j], f_lo[j] = split(v)
-        over_rows(low, high, body)
+                first[j] = v
+                two(f_two, j, v)
+            else:
+                x[base + j] = v
+
+    def postsmooth(cycle, base, n, halo, keep=False):
+        def body(ps):
+            js, products = [], []
+            for p in ps:
+                js += [2 + 2 * p, 3 + 2 * p]
+                products += a_pair(base, 2 + 2 * p, x_two)
+            settle(base, js, finish(cycle, base, js, products), keep)
+        if n > 1:
+            over_rows(0, n // 2, body, 2)
+        if halo:
+            js = [1, n + 2]
+            products = [a_single(base, 1, 0, x_two), a_single(base, n + 2, n, x_two)]
+            settle(base, js, finish(cycle, base, js, products), keep)
+        if n == 1:
+            settle(base, [2], finish(cycle, base, [2], [a_single(base, 2, 1, x_two)]), keep)
 
     def zero_rows(ref, indices):
         for i in indices:
@@ -225,32 +266,27 @@
         presmooth(cycle, base, 2, n + 2)
         for side in range(2):
             outer = (0, 1) if side == 0 else (n + 2, n + 3)
-            inner = 1 if side == 0 else n + 2
-
-            def arrive(side=side, outer=outer, inner=inner):
+
+            def arrive(side=side, outer=outer):
                 b_halo(cycle, l, side).wait_recv()
                 if cycle == 0:
                     o_halo(l, side, 0).wait_recv()
-                    o_halo(l, side, 1).wait_recv()
                     for t, j in enumerate(outer):
                         pack_s(base + j, raw_s[l, side, 0, t])
-                    pack_a(base + inner, raw_a[l, side, 0, 0], raw_a[l, side, 1, 0], raw_a[l, side, 2, 0])
 
             pl.when(has[side])(arrive)
             if cycle == 0:
-                def blank(outer=outer, inner=inner):
+                def blank(outer=outer):
                     for j in outer:
-                        s3[base + j] = jnp.zeros(s3.shape[1:], bf16)
+                        s4[base + j] = jnp.zeros(s4.shape[1:], bf16)
                         b[0, base + j] = jnp.zeros(b.shape[2:], f32)
                         b[1, base + j] = jnp.zeros(b.shape[2:], f32)
-                    a_hi[base + inner] = jnp.zeros(a_hi.shape[1:], bf16)
-                    a_lo[base + inner] = jnp.zeros(a_lo.shape[1:], bf16)
                 pl.when(jnp.logical_not(has[side]))(blank)
         js = [0, 1, n + 2, n + 3]
         values = [s_mul(base + j, b[cycle, base + j]) for j in js]
         for j, v in zip(js, values):
             x[base + j] = v
-            x_hi[j], x_lo[j] = split(v)
+            two(x_two, j, v)
         half = n // 2
         if l + 1 < levels:
             def store(p, c):
@@ -272,105 +308,129 @@
     def solve_wide(cycle):
         if cycle == 0:
             own = offsets[levels]
-            pack_a(gather_base + 2 + dev, raw[0, own], raw[1, own], raw[2, own])
-            pack_s(gather_base + 2 + dev, raw[3, own])
+            raw_g[dev] = raw[:, pl.ds(own, 1)]
             coarse_copy.wait()
-            first = 0
+            start = 0
             for m in range(1, len(wide)):
-                def body(js, first=first, m=m):
-                    for j in js:
-                        row = wide_bases[m] + 2 + j
-                        pack_a(row, raw_c[0, 0, first + j], raw_c[1, 0, first + j], raw_c[2, 0, first + j])
-                        pack_s(row, raw_c[3, 0, first + j])
-                over_rows(0, wide[m], body, 2)
-                first += wide[m]
-
-            def take(k, carry):
+                def body(ps, start=start, m=m):
+                    for p in ps:
+                        pack_pair(wide_bases[m], p, [
+                            [raw_c[k, 0, start + 2 * p + t] for k in range(4)] for t in range(2)])
+                if wide[m] > 1:
+                    over_rows(0, wide[m] // 2, body, 2)
+                else:
+                    row = wide_bases[m] + 2
+                    put(a_op, row, placed_a(False, *[raw_c[k, 0, start] for k in range(3)]))
+                    pack_s(row, raw_c[3, 0, start])
+                start += wide[m]
+            for k in range(1, devices):
                 sender = lax.rem(dev + k, devices)
                 go_copy(0, sender, sender).wait_recv()
-                row = gather_base + 2 + sender
-                pack_a(row, raw_g[sender, 0, 0], raw_g[sender, 1, 0], raw_g[sender, 2, 0])
-                pack_s(row, raw_g[sender, 3, 0])
-                return carry
-            lax.fori_loop(1, devices, take, 0)
-            zero_rows(e, [gather_base + 1, gather_base + wide[0] + 2])
+
+            def body(ps):
+                for p in ps:
+                    pack_pair(gather_base, p, [[raw_g[2 * p + t, k, 0] for k in range(4)] for t in range(2)])
+            over_rows(0, devices // 2, body, 2)
+            zero_rows(x, [gather_base + 1, gather_base + wide[0] + 2])
         for k in range(1, devices):
             sender = lax.rem(dev + k, devices)
             g_copy(cycle, 0, sender, sender).wait_recv()
 
         def visit(m):
             n, base = wide[m], wide_bases[m]
-            pads = [1, n + 2]
+            pads = [1, n + 2] + ([n + 3] if n == 1 else [])
             presmooth(cycle, base, 2, n + 2)
             if m + 1 < len(wide):
-                zero_rows(x_hi, pads)
-                zero_rows(x_lo, pads)
+                zero_rows(x_two, pads)
 
                 def store(p, c):
                     b[cycle, wide_bases[m + 1] + 2 + p] = c
                 restrict(cycle, base, [(0, n // 2)], store)
                 visit(m + 1)
                 correct(base, 2, n + 2, lambda i: wide_bases[m + 1] + i)
-            zero_rows(x_hi, pads)
-            zero_rows(x_lo, pads)
-            postsmooth(cycle, base, 2, n + 2)
+            zero_rows(x_two, pads)
+            postsmooth(cycle, base, n, False)
         visit(0)
 
     def up_to(cycle, l):
+        n, base = heights[l], bases[l]
         if l == levels - 1:
-            correct(bases[l], 0, heights[l] + 4, lambda i: gather_base + dev + i)
+            correct(base, 0, n + 4, lambda i: gather_base + dev + i)
         else:
-            correct(bases[l], 0, heights[l] + 4, lambda i: bases[l + 1] + i)
+            correct(base, 0, n + 4, lambda i: bases[l + 1] + i)
+        if cycle == 0:
+            for side in range(2):
+                row = base + (1 if side == 0 else n + 2)
+
+                def arrive(side=side, row=row):
+                    o_halo(l, side, 1).wait_recv()
+                    put(a_op, row, placed_a(side == 1, *[raw_a[l, side, k, 0] for k in range(3)]))
+
+                def blank(row=row):
+                    a_op[row] = jnp.zeros(a_op.shape[1:], bf16)
+                pl.when(has[side])(arrive)
+                pl.when(jnp.logical_not(has[side]))(blank)
 
     for l in range(levels):
         down_local(0, l)
     solve_wide(0)
     for l in reversed(range(levels)):
         up_to(0, l)
-        postsmooth(0, bases[l], 1, heights[l] + 3, keep=l == 0)
+        postsmooth(0, bases[l], heights[l], True, keep=l == 0)
 
     base = bases[0]
 
-    def again(js):
-        values = [b[0, base + j] - a_mul(base + j, j, f_hi, f_lo) for j in js]
+    def again(ps):
+        js, products = [], []
+        for p in ps:
+            js += [2 + 2 * p, 3 + 2 * p]
+            products += a_pair(base, 2 + 2 * p, f_two)
+        values = [b[0, base + j] - v for j, v in zip(js, products)]
         for j, v in zip(js, values):
             b[1, base + j] = v
-    again([2, 3, rows, rows + 1])
+    again([0, rows // 2 - 1])
     send_b(1, 0)
-    over_rows(4, rows, again)
+    over_rows(1, rows // 2 - 1, again, 2)
 
     for l in range(levels):
         down_local(1, l)
     solve_wide(1)
     for l in reversed(range(1, levels)):
         up_to(1, l)
-        postsmooth(1, bases[l], 1, heights[l] + 3)
+        postsmooth(1, bases[l], heights[l], True)
     up_to(1, 0)
 
     def slab_copy(k, slab, sender):
         return remote(staged.at[pl.ds(slab * per_slab, per_slab)], out.at[pl.ds(sender * per_slab, per_slab)],
                       t_send.at[k], t_recv.at[sender], "grp", slab)
 
-    steps = [(k + groups // 2) % groups for k in range(groups)]
-    steps = [k for k in steps if k] + [0]
-    for k in steps:
-        slab = lax.rem(grp + k, groups)
+    sent = []
+    for k in [k for k in range(groups) if k != groups // 2] + [groups // 2]:
+        slab = lax.rem(grp + groups // 2 + 2 * (k // 2), groups)
+        if k % 2:
+            slab = slab + 1 - 2 * lax.rem(slab, 2)
 
         def body(us, slab=slab):
             ts = [slab * per_slab + u for u in us]
             js = [order[0, t] + 2 for t in ts]
-            values = smoothed(1, base, js)
-            values = [v + e[base + j] for v, j in zip(values, js)]
+            products = []
+            for j in js:
+                low = j - 1 - lax.rem(j, 2)
+                products.append(a_single(base, j, low, x_two))
+            values = finish(1, base, js, products)
+            values = [v + first[j] for v, j in zip(values, js)]
             for t, v in zip(ts, values):
                 staged[t] = v
+        own = k == groups // 2
         over_rows(0, per_slab, body)
-        if k:
+        if own:
+            keep = pltpu.make_async_copy(staged.at[pl.ds(slab * per_slab, per_slab)],
+                                         out.at[pl.ds(grp * per_slab, per_slab)], local_sem.at[0])
+            keep.start()
+        else:
             slab_copy(k, slab, grp).start()
-        else:
-            own = pltpu.make_async_copy(staged.at[pl.ds(slab * per_slab, per_slab)],
-                                        out.at[pl.ds(grp * per_slab, per_slab)], local_sem.at[0])
-            own.start()
-            own.wait()
+            sent.append((k, slab))
+    keep.wait()
 
     for l in range(levels):
         for side in range(2):
@@ -385,8 +445,7 @@
         go_copy(k, dev, target).wait_send()
         g_copy(0, k, dev, target).wait_send()
         g_copy(1, k, dev, target).wait_send()
-    for k in range(1, groups):
-        slab = lax.rem(grp + k, groups)
+    for k, slab in sent:
         slab_copy(k, slab, grp).wait_send()
         slab_copy(k, slab, slab).wait_recv()
 
@@ -414,16 +473,14 @@
         pltpu.VMEM((levels, 2, 3, 1, size, size), f32),
         pltpu.VMEM((devices, kinds, 1, size, size), f32),
         pltpu.VMEM(coarse_ops.shape, f32),
-        pltpu.VMEM((total, size, 3 * size), bf16),
-        pltpu.VMEM((total, size, 3 * size), bf16),
-        pltpu.VMEM((total, size, 3 * size), bf16),
+        pltpu.VMEM((total, 2 * size, 4 * size), bf16),
+        pltpu.VMEM((total // 2 + 1, 2 * size, 4 * size), bf16),
+        pltpu.VMEM((total, size, 4 * size), bf16),
         pltpu.VMEM((2, total, size, cases), f32),
         pltpu.VMEM((total, size, cases), f32),
-        pltpu.VMEM((total, size, cases), f32),
-        pltpu.VMEM((most, size, cases), bf16),
-        pltpu.VMEM((most, size, cases), bf16),
-        pltpu.VMEM((rows + 4, size, cases), bf16),
-        pltpu.VMEM((rows + 4, size, cases), bf16),
+        pltpu.VMEM((rows + 4, size, cases), f32),
+        pltpu.VMEM((most, size, 2 * cases), bf16),
+        pltpu.VMEM((rows + 4, size, 2 * cases), bf16),
         pltpu.VMEM((rows, size, cases), f32),
         dma((CHUNKS + 3,)),
         dma((2, levels, 2)), dma((2, levels, 2)),

time: 132 us -> 126 us (0.955)
  Pallas kernels: 129 us -> 124 us
    pallas_call x1, Pallas kernels: 129 us -> 124 us  [shards(): pl.pallas_call(functools.partial(kernel, plan), out_shape=jax.ShapeDtypeS...]
where the time goes in v1:
time: 126 us
  Pallas kernels  124 us (98%)
  local copies, waits for them, and re-layouts  2.31 us (2%)
    pallas_call x1, Pallas kernels, shards(): pl.pallas_call(functools.partial(kernel, plan), out_shape=jax.ShapeDtypeS...  124 us

profile of v1, /device:TPU:10, one launch (start us, length us, event | category | flops | bytes accessed | tf_op | source)
XLA Modules:
  0.0 126.0 jit_solution(10562733248280114141)
XLA Ops:
  0.0 123.7 %shard_map.46 = f32[32,64,128]{2,1,0:T(8,128)} custom-call(f32[32,64,128]{2,1,0:T(8,128)} %load.1, f32[4,63,64,64]{3,2,1,0:T(8,128)} %ops.1, f32[4,1,7,64,64]{4,3,2,1,0:T(8,128)} %coarse.1, s32[1,32]{1,0:T(1,128)} %order.1), custom_call_target="tpu_custom_call" | custom-call | tf_op jit(solution)/shard_map/pallas_call | solution.py:493
  123.7 2.3 %copy.6 = f32[32,64,128]{2,1,0:T(8,128)} copy(f32[32,64,128]{2,1,0:T(8,128)} %shard_map.46) | data formatting | bytes 2097152

commit v2 on v1

--- a/solution.py
+++ b/solution.py
@@ -193,7 +193,7 @@
             for j, v in zip(js, values):
                 x[base + j] = v
                 two(x_two, j, v)
-        over_rows(low, high, body, 8)
+        over_rows(low, high, body, 16)
 
     def restrict(cycle, base, pairs, store):
         def body(ps):
@@ -204,8 +204,10 @@
                 values.append(0.5 * (b[cycle, base + j] + b[cycle, base + j + 1]) - gathered(product))
             for p, v in zip(ps, values):
                 store(p, v)
-        for low, high in pairs:
-            over_rows(low, high, body, 4)
+        if isinstance(pairs, list):
+            body(pairs)
+        else:
+            over_rows(*pairs, body, 6)
 
     def correct(base, low, high, e_row):
         def body(ps):
@@ -217,7 +219,7 @@
             for j, v in zip(js, vs):
                 x[base + j] = v
                 two(x_two, j, v)
-        over_rows(low // 2, high // 2, body, 2)
+        over_rows(low // 2, high // 2, body, 6)
 
     def finish(cycle, base, js, products):
         r = [b[cycle, base + j] - v for j, v in zip(js, products)]
@@ -232,20 +234,21 @@
                 x[base + j] = v
 
     def postsmooth(cycle, base, n, halo, keep=False):
-        def body(ps):
+        def body(ps, singles=()):
             js, products = [], []
             for p in ps:
                 js += [2 + 2 * p, 3 + 2 * p]
                 products += a_pair(base, 2 + 2 * p, x_two)
-            settle(base, js, finish(cycle, base, js, products), keep)
-        if n > 1:
-            over_rows(0, n // 2, body, 2)
-        if halo:
-            js = [1, n + 2]
-            products = [a_single(base, 1, 0, x_two), a_single(base, n + 2, n, x_two)]
+            for j, low in singles:
+                js.append(j)
+                products.append(a_single(base, j, low, x_two))
             settle(base, js, finish(cycle, base, js, products), keep)
         if n == 1:
-            settle(base, [2], finish(cycle, base, [2], [a_single(base, 2, 1, x_two)]), keep)
+            body([], [(2, 1)])
+            return
+        head = max(0, (n // 2 - 1) // 4 * 4)
+        over_rows(0, head, body, 4)
+        body(list(range(head, n // 2)), [(1, 0), (n + 2, n)] if halo else [])
 
     def zero_rows(ref, indices):
         for i in indices:
@@ -292,16 +295,16 @@
             def store(p, c):
                 b[cycle, bases[l + 1] + 2 + p] = c
             if half > 4:
-                restrict(cycle, base, [(0, 2), (half - 2, half)], store)
+                restrict(cycle, base, [0, 1, half - 2, half - 1], store)
                 send_b(cycle, l + 1)
-                restrict(cycle, base, [(2, half - 2)], store)
+                restrict(cycle, base, (2, half - 2), store)
             else:
-                restrict(cycle, base, [(0, half)], store)
+                restrict(cycle, base, (0, half), store)
                 send_b(cycle, l + 1)
         else:
             def store(p, c):
                 b[cycle, gather_base + 2 + dev] = c
-            restrict(cycle, base, [(0, half)], store)
+            restrict(cycle, base, (0, half), store)
             for k in range(1, devices):
                 g_copy(cycle, k, dev, lax.rem(dev + k, devices)).start()
 
@@ -345,7 +348,7 @@
 
                 def store(p, c):
                     b[cycle, wide_bases[m + 1] + 2 + p] = c
-                restrict(cycle, base, [(0, n // 2)], store)
+                restrict(cycle, base, (0, n // 2), store)
                 visit(m + 1)
                 correct(base, 2, n + 2, lambda i: wide_bases[m + 1] + i)
             zero_rows(x_two, pads)
@@ -390,7 +393,7 @@
             b[1, base + j] = v
     again([0, rows // 2 - 1])
     send_b(1, 0)
-    over_rows(1, rows // 2 - 1, again, 2)
+    over_rows(1, rows // 2 - 1, again, 4)
 
     for l in range(levels):
         down_local(1, l)
@@ -422,7 +425,7 @@
             for t, v in zip(ts, values):
                 staged[t] = v
         own = k == groups // 2
-        over_rows(0, per_slab, body)
+        over_rows(0, per_slab, body, 8)
         if own:
             keep = pltpu.make_async_copy(staged.at[pl.ds(slab * per_slab, per_slab)],
                                          out.at[pl.ds(grp * per_slab, per_slab)], local_sem.at[0])

time: 126 us -> 119 us (0.944)
  Pallas kernels: 124 us -> 116 us
    pallas_call x1, Pallas kernels: 124 us -> 116 us  [shards(): pl.pallas_call(functools.partial(kernel, plan), out_shape=jax.ShapeDtypeS...]
where the time goes in v2:
time: 119 us; the launch traced here: 118 us
  Pallas kernels  116 us (97%)
  local copies, waits for them, and re-layouts  2.31 us (2%)
    pallas_call x1, Pallas kernels, shards(): pl.pallas_call(functools.partial(kernel, plan), out_shape=jax.ShapeDtypeS...  116 us

profile of v2, /device:TPU:10, one launch (start us, length us, event | category | flops | bytes accessed | tf_op | source)
XLA Modules:
  0.0 118.4 jit_solution(7055587111791663729)
XLA Ops:
  0.0 116.1 %shard_map.46 = f32[32,64,128]{2,1,0:T(8,128)} custom-call(f32[32,64,128]{2,1,0:T(8,128)} %load.1, f32[4,63,64,64]{3,2,1,0:T(8,128)} %ops.1, f32[4,1,7,64,64]{4,3,2,1,0:T(8,128)} %coarse.1, s32[1,32]{1,0:T(1,128)} %order.1), custom_call_target="tpu_custom_call" | custom-call | tf_op jit(solution)/shard_map/pallas_call | solution.py:496
  116.1 2.3 %copy.6 = f32[32,64,128]{2,1,0:T(8,128)} copy(f32[32,64,128]{2,1,0:T(8,128)} %shard_map.46) | data formatting | bytes 2097152

commit v3 on v2

--- a/solution.py
+++ b/solution.py
@@ -119,14 +119,12 @@
         return remote(row, row, g_send.at[cycle, k], g_recv.at[cycle, sender], "dev", target)
 
     send_b(0, 0)
-    for l in range(levels):
-        for side in range(2):
-            def begin(side=side, l=l):
-                o_halo(l, side, 0).start()
-                o_halo(l, side, 1).start()
-            on_send(side, begin)
-    for k in range(1, devices):
-        go_copy(k, dev, lax.rem(dev + k, devices)).start()
+    def send_o(part, these):
+        for l in these:
+            for side in range(2):
+                on_send(side, lambda l=l, side=side: o_halo(l, side, part).start())
+
+    send_o(0, [0])
 
     size = x.shape[1]
     cases = x.shape[2]
@@ -262,6 +260,8 @@
                 for c in range(CHUNKS):
                     fine_copies[c].wait()
                     pack_own(0, c * piece, (c + 1) * piece)
+                    if c == 0:
+                        send_o(0, range(1, levels))
             else:
                 if l == 1:
                     rest_copy.wait()
@@ -297,10 +297,15 @@
             if half > 4:
                 restrict(cycle, base, [0, 1, half - 2, half - 1], store)
                 send_b(cycle, l + 1)
+                if cycle == 0 and l == 0:
+                    for k in range(1, devices):
+                        go_copy(k, dev, lax.rem(dev + k, devices)).start()
                 restrict(cycle, base, (2, half - 2), store)
             else:
                 restrict(cycle, base, (0, half), store)
                 send_b(cycle, l + 1)
+            if cycle == 0 and l == 1:
+                send_o(1, reversed(range(levels)))
         else:
             def store(p, c):
                 b[cycle, gather_base + 2 + dev] = c

time: 119 us -> 114 us (0.958)
  Pallas kernels: 116 us -> 111 us
    pallas_call x1, Pallas kernels: 116 us -> 111 us  [shards(): pl.pallas_call(functools.partial(kernel, plan), out_shape=jax.ShapeDtypeS...]
where the time goes in v3:
time: 114 us
  Pallas kernels  111 us (97%)
  local copies, waits for them, and re-layouts  2.31 us (2%)
    pallas_call x1, Pallas kernels, shards(): pl.pallas_call(functools.partial(kernel, plan), out_shape=jax.ShapeDtypeS...  111 us
    unnamed x1, local copies, waits for them, and re-layouts  2.31 us

profile of v3, /device:TPU:10, one launch (start us, length us, event | category | flops | bytes accessed | tf_op | source)
XLA Modules:
  0.0 113.6 jit_solution(8539297402252773200)
XLA Ops:
  0.0 111.2 %shard_map.46 = f32[32,64,128]{2,1,0:T(8,128)} custom-call(f32[32,64,128]{2,1,0:T(8,128)} %load.1, f32[4,63,64,64]{3,2,1,0:T(8,128)} %ops.1, f32[4,1,7,64,64]{4,3,2,1,0:T(8,128)} %coarse.1, s32[1,32]{1,0:T(1,128)} %order.1), custom_call_target="tpu_custom_call" | custom-call | tf_op jit(solution)/shard_map/pallas_call | solution.py:501
  111.2 2.3 %copy.6 = f32[32,64,128]{2,1,0:T(8,128)} copy(f32[32,64,128]{2,1,0:T(8,128)} %shard_map.46) | data formatting | bytes 2097152

commit v4 on v3

--- a/solution.py
+++ b/solution.py
@@ -36,7 +36,7 @@
     load, ops, coarse, order,
     out,
     raw, raw_s, raw_a, raw_g, raw_c,
-    a_op, r_op, s4, b, x, first, x_two, f_two, staged,
+    a_op, r_op, s4, d_op, b, x, first, x_two, f_two, staged,
     local_sem, b_send, b_recv, o_send, o_recv, go_send, go_recv, g_send, g_recv, t_send, t_recv,
 ):
     devices, groups, heights, bases, wide, wide_bases = plan
@@ -166,7 +166,8 @@
         return jnp.dot(s4[row], jnp.concatenate([hi, lo, hi, lo], axis=0), preferred_element_type=f32)
 
     def gathered(product):
-        upper, lower = product[:size], product[size:]
+        half = product.shape[0] // 2
+        upper, lower = product[:half], product[half:]
         return (lower[:, cases:] + (upper[:, cases:] + lower[:, :cases])) + upper[:, :cases]
 
     def window(ref, low):
@@ -251,6 +252,56 @@
     def zero_rows(ref, indices):
         for i in indices:
             ref[i] = jnp.zeros(ref.shape[1:], ref.dtype)
+
+    dense = wide.index(2) if 2 in wide[1:] and 2 * size == cases else None
+
+    def pack_coarse():
+        coarse_copy.wait()
+        start = 0
+        for m in range(1, len(wide)):
+            def body(ps, start=start, m=m):
+                for p in ps:
+                    pack_pair(wide_bases[m], p, [
+                        [raw_c[k, 0, start + 2 * p + t] for k in range(4)] for t in range(2)])
+            if wide[m] > 1:
+                over_rows(0, wide[m] // 2, body, 2)
+            else:
+                row = wide_bases[m] + 2
+                put(a_op, row, placed_a(False, *[raw_c[k, 0, start] for k in range(3)]))
+                pack_s(row, raw_c[3, 0, start])
+            start += wide[m]
+
+    def visit(cycle, m, direct=True):
+        n, base = wide[m], wide_bases[m]
+        if direct and m == dense:
+            high, low = split(b[cycle, pl.ds(base + 2, 2)].reshape(2 * size, cases))
+            value = gathered(jnp.dot(d_op[...], jnp.concatenate([high, low], axis=1), preferred_element_type=f32))
+            x[base + 2] = value[:size]
+            x[base + 3] = value[size:]
+            return
+        pads = [1, n + 2] + ([n + 3] if n == 1 else [])
+        presmooth(cycle, base, 2, n + 2)
+        if m + 1 < len(wide):
+            zero_rows(x_two, pads)
+
+            def store(p, c):
+                b[cycle, wide_bases[m + 1] + 2 + p] = c
+            restrict(cycle, base, (0, n // 2), store)
+            visit(cycle, m + 1)
+            correct(base, 2, n + 2, lambda i: wide_bases[m + 1] + i)
+        zero_rows(x_two, pads)
+        postsmooth(cycle, base, n, False)
+
+    def form_dense():
+        base = wide_bases[dense]
+        shape = (2 * size, cases)
+        unit = (lax.broadcasted_iota(jnp.int32, shape, 0) == lax.broadcasted_iota(jnp.int32, shape, 1)).astype(f32)
+        b[0, base + 2] = unit[:size]
+        b[0, base + 3] = unit[size:]
+        visit(0, dense, False)
+        hi, lo = split(x[pl.ds(base + 2, 2)].reshape(shape))
+        d_op[pl.ds(0, 2 * size)] = hi
+        d_op[pl.ds(2 * size, 2 * size)] = lo
 
     def down_local(cycle, l):
         n, base = heights[l], bases[l]
@@ -306,6 +357,9 @@
                 send_b(cycle, l + 1)
             if cycle == 0 and l == 1:
                 send_o(1, reversed(range(levels)))
+                pack_coarse()
+                if dense is not None:
+                    form_dense()
         else:
             def store(p, c):
                 b[cycle, gather_base + 2 + dev] = c
@@ -317,20 +371,6 @@
         if cycle == 0:
             own = offsets[levels]
             raw_g[dev] = raw[:, pl.ds(own, 1)]
-            coarse_copy.wait()
-            start = 0
-            for m in range(1, len(wide)):
-                def body(ps, start=start, m=m):
-                    for p in ps:
-                        pack_pair(wide_bases[m], p, [
-                            [raw_c[k, 0, start + 2 * p + t] for k in range(4)] for t in range(2)])
-                if wide[m] > 1:
-                    over_rows(0, wide[m] // 2, body, 2)
-                else:
-                    row = wide_bases[m] + 2
-                    put(a_op, row, placed_a(False, *[raw_c[k, 0, start] for k in range(3)]))
-                    pack_s(row, raw_c[3, 0, start])
-                start += wide[m]
             for k in range(1, devices):
                 sender = lax.rem(dev + k, devices)
                 go_copy(0, sender, sender).wait_recv()
@@ -344,21 +384,7 @@
             sender = lax.rem(dev + k, devices)
             g_copy(cycle, 0, sender, sender).wait_recv()
 
-        def visit(m):
-            n, base = wide[m], wide_bases[m]
-            pads = [1, n + 2] + ([n + 3] if n == 1 else [])
-            presmooth(cycle, base, 2, n + 2)
-            if m + 1 < len(wide):
-                zero_rows(x_two, pads)
-
-                def store(p, c):
-                    b[cycle, wide_bases[m + 1] + 2 + p] = c
-                restrict(cycle, base, (0, n // 2), store)
-                visit(m + 1)
-                correct(base, 2, n + 2, lambda i: wide_bases[m + 1] + i)
-            zero_rows(x_two, pads)
-            postsmooth(cycle, base, n, False)
-        visit(0)
+        visit(cycle, 0)
 
     def up_to(cycle, l):
         n, base = heights[l], bases[l]
@@ -484,6 +510,7 @@
         pltpu.VMEM((total, 2 * size, 4 * size), bf16),
         pltpu.VMEM((total // 2 + 1, 2 * size, 4 * size), bf16),
         pltpu.VMEM((total, size, 4 * size), bf16),
+        pltpu.VMEM((4 * size, cases), bf16),
         pltpu.VMEM((2, total, size, cases), f32),
         pltpu.VMEM((total, size, cases), f32),
         pltpu.VMEM((rows + 4, size, cases), f32),

time: 114 us -> 112 us (0.982)
  Pallas kernels: 111 us -> 109 us
    pallas_call x1, Pallas kernels: 111 us -> 109 us  [shards(): pl.pallas_call(functools.partial(kernel, plan), out_shape=jax.ShapeDtypeS...]
where the time goes in v4:
time: 112 us
  Pallas kernels  109 us (97%)
  local copies, waits for them, and re-layouts  2.31 us (2%)
    pallas_call x1, Pallas kernels, shards(): pl.pallas_call(functools.partial(kernel, plan), out_shape=jax.ShapeDtypeS...  109 us
    unnamed x1, local copies, waits for them, and re-layouts  2.31 us

profile of v4, /device:TPU:10, one launch (start us, length us, event | category | flops | bytes accessed | tf_op | source)
XLA Modules:
  0.0 111.6 jit_solution(17743210390178047134)
XLA Ops:
  0.0 109.3 %shard_map.46 = f32[32,64,128]{2,1,0:T(8,128)} custom-call(f32[32,64,128]{2,1,0:T(8,128)} %load.1, f32[4,63,64,64]{3,2,1,0:T(8,128)} %ops.1, f32[4,1,7,64,64]{4,3,2,1,0:T(8,128)} %coarse.1, s32[1,32]{1,0:T(1,128)} %order.1), custom_call_target="tpu_custom_call" | custom-call | tf_op jit(solution)/shard_map/pallas_call | solution.py:528
  109.3 2.3 %copy.6 = f32[32,64,128]{2,1,0:T(8,128)} copy(f32[32,64,128]{2,1,0:T(8,128)} %shard_map.46) | data formatting | bytes 2097152
